TPU v7x, 768 devices: a whole 4x8x12 slice. The times are simulated.
768 devices in a mesh: wide: 48 (over x, z), narrow: 16 (over y, core).
Axes of the slice: x: 4, y: 8, z: 12, core: 2. Of those that a mesh axis runs over, the one named last changes fastest.
Arguments:
- agg_rows: bfloat16 [6144, 3840], P('wide'), may hold values from -6 to 6
- seed_feats: bfloat16 [6144, 768], P('wide'), may hold values from -6 to 6
- seed_type: int32 [6144], P('wide'), may hold values from 0 to 1
- w_rel: bfloat16 [3840, 1024], P(None, 'narrow'), may hold values from -0.09375 to 0.09375
- w_self: bfloat16 [2, 768, 1024], P(None, None, 'narrow'), may hold values from -0.21875 to 0.21875
- cotangent: float32 [6144, 1024], P('wide', 'narrow'), may hold values from -6 to 6
- counts: int32 [6144, 5], P('wide'), may hold values from 1 to 25
- owner: int32 [768000, 1], P('wide'), may hold values from 0 to 47; in each aligned block of 1000 rows (0 to 999, 1000 to 1999, ...) at most 26 rows name the same one
- local_row: int32 [768000], P('wide'), may hold values from 0 to 511
Outputs:
- table_grad: float32 [24576, 768], P('wide')
- grad_rel: float32 [3840, 1024], P(None, 'narrow')
- grad_self: float32 [2, 768, 1024], P(None, None, 'narrow')
Inputs may be any that keep to these rules, and one draw needn't show every extreme that they name: In each aligned block of 1000 slots no owner appears more than 26 times, and some owner appears exactly 26 times in some block; every owner appears somewhere.
All inputs are finite; a program needn't handle non-finite values.
Results may differ from a plain program's by a relative error of at most 0.0041.
Values may be sent and summed in bfloat16 or wider, within the bound.
A program may use at most 64 MiB of HBM per device.

v0:
```python
import jax
import jax.numpy as jnp
from jax import lax
from jax.sharding import PartitionSpec as P

FAN = 25
NODES_DEV = 512


def pack_slots(message, live_count, slot_owner, slot_row, blocks, per_block, owners):
    seeds_here, relations, width = message.shape
    fan_iota = lax.broadcasted_iota(jnp.int32, (1, 1, FAN), 2)
    live = fan_iota < live_count[:, :, None]
    values = jnp.where(live[:, :, :, None], message[:, :, None, :], jnp.zeros((), jnp.bfloat16))
    values = values.reshape(seeds_here * relations * FAN, width)
    onehot = (slot_owner[:, None] == lax.broadcasted_iota(jnp.int32, (1, owners), 1)).astype(
        jnp.int32
    )
    onehot = onehot.reshape(blocks, -1, owners)
    before = jnp.cumsum(onehot, axis=1) - onehot
    rank = jnp.sum(before * onehot, axis=2)
    block_ids = lax.broadcasted_iota(jnp.int32, rank.shape, 0)
    places = slot_owner * (blocks * per_block) + (block_ids * per_block + rank).reshape(-1)
    total = owners * blocks * per_block
    buffer = jnp.zeros((total, width), jnp.bfloat16).at[places].set(values)
    targets = jnp.zeros((total,), jnp.int32).at[places].set(slot_row)
    return (
        buffer.reshape(owners, blocks * per_block, width),
        targets.reshape(owners, blocks * per_block),
    )


def accumulate(received, targets, nodes_here):
    width = received.shape[2]
    table = jnp.zeros((nodes_here, width), jnp.float32)
    return table.at[targets.reshape(-1)].add(received.reshape(-1, width).astype(jnp.float32))


def sum_weights(rel_local, self_local):
    return lax.psum((rel_local, self_local), "wide")


def body(agg_rows, seed_feats, seed_type, w_rel, w_self, cotangent, counts, owner, local_row):
    seeds_here = agg_rows.shape[0]
    feat_width = seed_feats.shape[1]
    relations = counts.shape[1]
    owners = lax.axis_size("wide")
    groups = lax.axis_size("narrow")
    nodes_here = NODES_DEV
    pre_rel = jnp.dot(agg_rows, w_rel, preferred_element_type=jnp.float32)
    self_zero = jnp.dot(seed_feats, w_self[0], preferred_element_type=jnp.float32)
    self_one = jnp.dot(seed_feats, w_self[1], preferred_element_type=jnp.float32)
    pre = pre_rel + jnp.where(seed_type[:, None] == 0, self_zero, self_one)
    sigma = jax.nn.sigmoid(pre)
    dpre = (cotangent * sigma * (1.0 + pre * (1.0 - sigma))).astype(jnp.bfloat16)
    dims = (((0,), (0,)), ((), ()))
    rel_local = lax.dot_general(agg_rows, dpre, dims, preferred_element_type=jnp.float32)
    zero_b = jnp.zeros_like(dpre)
    self_local = jnp.stack(
        [
            lax.dot_general(
                seed_feats,
                jnp.where(seed_type[:, None] == t, dpre, zero_b),
                dims,
                preferred_element_type=jnp.float32,
            )
            for t in range(w_self.shape[0])
        ]
    )
    grad_rel, grad_self = sum_weights(rel_local, self_local)
    d_part = lax.dot_general(
        dpre, w_rel, (((1,), (1,)), ((), ())), preferred_element_type=jnp.float32
    )
    d_part = d_part.reshape(seeds_here, relations, feat_width)
    block = seeds_here * relations * FAN // groups
    per_block = 5 * block // (4 * owners)
    slot_owner = owner[:, 0]
    d_agg = lax.psum_scatter(d_part, "narrow", scatter_dimension=0, tiled=True)
    my_group = lax.axis_index("narrow")
    seeds_mine = seeds_here // groups
    live_count = lax.dynamic_slice_in_dim(counts, my_group * seeds_mine, seeds_mine, 0)
    message = (d_agg / live_count[:, :, None].astype(jnp.float32)).astype(jnp.bfloat16)
    my_owner = lax.dynamic_slice_in_dim(slot_owner, my_group * block, block, 0)
    my_rows = lax.dynamic_slice_in_dim(local_row, my_group * block, block, 0)
    buffer, targets = pack_slots(message, live_count, my_owner, my_rows, 1, per_block, owners)
    received, got_rows = (
        lax.all_to_all(buffer, "wide", split_axis=0, concat_axis=0, tiled=True),
        lax.all_to_all(targets, "wide", split_axis=0, concat_axis=0, tiled=True),
    )
    partial_table = accumulate(received, got_rows, nodes_here)
    table_grad = lax.psum(partial_table, "narrow")
    return (table_grad, grad_rel, grad_self)


def solution(mesh):
    in_specs = (
        P("wide", None),
        P("wide", None),
        P("wide"),
        P(None, "narrow"),
        P(None, None, "narrow"),
        P("wide", "narrow"),
        P("wide", None),
        P("wide", None),
        P("wide"),
    )
    out_specs = (P("wide", None), P(None, "narrow"), P(None, None, "narrow"))
    return jax.shard_map(body, mesh=mesh, in_specs=in_specs, out_specs=out_specs, check_vma=False)
```

profile of v0, /device:TPU:1, one launch (start us, length us, event | category | flops | bytes accessed | tf_op | source)
XLA Modules:
  0.0 517.0 jit_solution(18433564892446292780)
XLA Ops:
  8.1 1.3 broadcast_compare_fusion
  9.3 1.2 fusion.10
  10.5 1.2 convolution_select_fusion
  11.7 1.5 multiply_convert_fusion
  13.8 2.3 copy.24
  17.0 13.5 %reduce-window.6 = s32[1,48,8,128]{3,2,1,0:T(8,128)S(1)} reduce-window(s32[1,48,8,128]{3,2,1,0:T(8,128)S(1)} %bitcast.46, s32[]{:T(128)} %constant.14.clone.1), window={size=1x1x1x128 pad=0_0x0_0x0_0x127_0}, to_apply=%region_0.1 | reduce-window | flops 6242304 | bytes 393220 | tf_op jit(solution)/shard_map/reduce-window
  32.8 5.3 %scatter_custom_fusion = s32[1248]{0:T(1024)S(1)} fusion(s32[1000]{0:T(1024)S(1)} %bitcast.51, s32[1000]{0:T(1024)S(1)} %dynamic_slice.10, s32[]{:T(128)} %constant.14.clone.1), kind=kCustom, calls=%fused_computation.41 | custom fusion | bytes 4996 | tf_op jit(solution)/shard_map/scatter | solution.py:26
  38.8 18.8 %all-to-all-start = ((s32[48,1,26]{2,1,0:T(1,128)}), s32[48,1,26]{2,1,0:T(1,128)S(1)}, u32[]{:S(2)}, u32[]{:S(2)}) async-start(s32[48,1,26]{2,1,0:T(1,128)} %bitcast.7), calls=%async_computation | async-start | bytes 49152 | tf_op jit(solution)/shard_map/all_to_all | solution.py:88
  58.1 31.1 %reduce-scatter.2.cloned.1.call-done = f32[8,5,768]{2,1,0:T(8,128)} async-done(((f32[128,5,768]{2,1,0:T(8,128)}), f32[8,5,768]{2,1,0:T(8,128)}) %reduce-scatter.2.cloned.1.call-update) | async-done | bytes 122896 | tf_op jit(solution)/shard_map/reduce_scatter | solution.py:78
  89.1 1.0 divide_convert_fusion
  90.3 1.6 broadcast_in_dim.66
  91.9 9.9 %scatter_custom_fusion.1 = bf16[1248,768]{1,0:T(8,128)(2,1)S(1)} fusion(s32[1000]{0:T(1024)S(1)} %bitcast.52, bf16[1000,768]{1,0:T(8,128)(2,1)} %broadcast_in_dim.66, pred[1000]{0:T(1024)(128)(4,1)S(1)} %lt.49, bf16[]{:T(256)} %constant.6.clone.1), kind=kCustom, calls=%fused_computation.4 | custom fusion | flops 768000 | bytes 3454976 | tf_op jit(solution)/shard_map/scatter | solution.py:25
  101.8 2.1 reshape.182
  104.6 11.1 %all-to-all-start.1 = ((bf16[48,26,768]{2,1,0:T(8,128)(2,1)}), bf16[48,26,768]{2,1,0:T(8,128)(2,1)S(1)}, u32[]{:S(2)}, u32[]{:S(2)}) async-start(bf16[48,26,768]{2,1,0:T(8,128)(2,1)} %reshape.182), calls=%async_computation.2 | async-start | bytes 4718592 | tf_op jit(solution)/shard_map/all_to_all | solution.py:87
  115.8 0.8 convolution_bitcast_fusion.2
  116.6 0.8 convolution_bitcast_fusion.1
  118.2 1.2 convolution_bitcast_fusion
  121.0 74.6 %all-to-all-done.1 = bf16[48,26,768]{2,1,0:T(8,128)(2,1)S(1)} async-done(((bf16[48,26,768]{2,1,0:T(8,128)(2,1)}), bf16[48,26,768]{2,1,0:T(8,128)(2,1)S(1)}, u32[]{:S(2)}, u32[]{:S(2)}) %all-to-all-start.1) | async-done | bytes 1916960 | tf_op jit(solution)/shard_map/all_to_all | solution.py:87
  195.5 2.5 reshape.204
  198.0 12.4 %scatter_custom_fusion.2 = f32[512,768]{1,0:T(8,128)} fusion(s32[1248]{0:T(1024)S(1)} %fusion.20, f32[1248,768]{1,0:T(8,128)} %reshape.204, f32[]{:T(128)} %constant.13.clone.1), kind=kCustom, calls=%fused_computation.12 | custom fusion | flops 958464 | bytes 1573376 | tf_op jit(solution)/shard_map/scatter-add | solution.py:36
  210.5 165.3 %all-reduce.7.cloned.1.call-done = (f32[3840,64]{0,1:T(8,128)}, f32[2,768,64]{1,2,0:T(8,128)}) async-done(((f32[3840,64]{0,1:T(8,128)}, f32[2,768,64]{1,2,0:T(8,128)}), (f32[3840,64]{0,1:T(8,128)}, f32[2,768,64]{1,2,0:T(8,128)})) %all-reduce.7.cloned.1.call-update) | async-done | bytes 1376272 | tf_op jit(solution)/shard_map/psum | solution.py:40
  375.7 129.4 %all-reduce.5.cloned.1.call-done = f32[512,768]{1,0:T(8,128)} async-done(((f32[512,768]{1,0:T(8,128)}), f32[512,768]{1,0:T(8,128)}) %all-reduce.5.cloned.1.call-update) | async-done | bytes 1572880 | tf_op jit(solution)/shard_map/psum | solution.py:91
  505.1 2.7 copy.31
  507.8 0.9 copy.32
  (55 shorter events, 8.6 us)
Async XLA Ops:
  8.0 3.7 copy-start
  8.0 5.3 %copy-start.2 = (bf16[3840,64]{0,1:T(8,128)(2,1)S(1)}, bf16[3840,64]{0,1:T(8,128)(2,1)}, u32[]{:S(2)}) copy-start(bf16[3840,64]{0,1:T(8,128)(2,1)} %param.12) | copy-start | bytes 1474564
  8.0 81.1 %reduce-scatter.2.cloned.1.call-start = ((), (), s32[]{:S(2)}) async-start(), calls=%async_computation.3 | async-start | bytes 3342336 | tf_op jit(solution)/shard_map/reduce_scatter | solution.py:78
  9.3 1.2 copy-start.8
  17.0 40.7 %copy-start.7 = (s32[128,5]{0,1:T(8,128)S(1)}, s32[128,5]{0,1:T(8,128)}, u32[]{:S(2)}) copy-start(s32[128,5]{0,1:T(8,128)} %param.15) | copy-start | bytes 7684
  38.8 65.2 %all-to-all-start = ((s32[48,1,26]{2,1,0:T(1,128)}), s32[48,1,26]{2,1,0:T(1,128)S(1)}, u32[]{:S(2)}, u32[]{:S(2)}) async-start(s32[48,1,26]{2,1,0:T(1,128)} %bitcast.7), calls=%async_computation | async-start | bytes 49152 | tf_op jit(solution)/shard_map/all_to_all | solution.py:88
  104.0 11.8 %copy-start.1 = (bf16[128,768]{1,0:T(8,128)(2,1)S(1)}, bf16[128,768]{1,0:T(8,128)(2,1)}, u32[]{:S(2)}) copy-start(bf16[128,768]{1,0:T(8,128)(2,1)} %param.10) | copy-start | bytes 589828
  104.0 0.6 copy-start.5
  104.6 91.0 %all-to-all-start.1 = ((bf16[48,26,768]{2,1,0:T(8,128)(2,1)}), bf16[48,26,768]{2,1,0:T(8,128)(2,1)S(1)}, u32[]{:S(2)}, u32[]{:S(2)}) async-start(bf16[48,26,768]{2,1,0:T(8,128)(2,1)} %reshape.182), calls=%async_computation.2 | async-start | bytes 4718592 | tf_op jit(solution)/shard_map/all_to_all | solution.py:87
  115.7 260.0 %all-reduce.7.cloned.1.call-start = ((), (), s32[]{:S(2)}) async-start(), calls=%async_computation.5 | async-start | bytes 2752512 | tf_op jit(solution)/shard_map/psum | solution.py:40
  117.4 2.8 copy-start.6
  119.4 385.7 %all-reduce.5.cloned.1.call-start = ((), (), s32[]{:S(2)}) async-start(), calls=%async_computation.4 | async-start | bytes 3145728 | tf_op jit(solution)/shard_map/psum | solution.py:91
  375.7 132.1 %copy-start.3 = (f32[3840,64]{0,1:T(8,128)S(1)}, f32[3840,64]{0,1:T(8,128)}, u32[]{:S(2)}) copy-start(f32[3840,64]{0,1:T(8,128)} %get-tuple-element.10) | copy-start | bytes 2949124
  505.1 3.7 copy-start.4
Sparse Core Ops, SparseCore 0:
  16.3 72.8 reduce-scatter.1
Sparse Core Ops, SparseCore 1:
  120.4 255.3 all-reduce.6
  378.5 126.5 all-reduce.4
where the time goes:
time: 517 us
  waiting for transfers between devices  400 us (77%)
  other arithmetic  40.6 us (8%)
  starting transfers between devices  30.3 us (6%)
  local copies, waits for them, and re-layouts  22.8 us (4%)
  between operations  15.8 us (3%)
  matrix products  7.22 us (1%)
    psum x1, waiting for transfers between devices, sum_weights(): return lax.psum((rel_local, self_local), 'wide')  165 us
    psum x1, waiting for transfers between devices, body(): table_grad = lax.psum(partial_table, 'narrow')  129 us
    all_to_all x1, waiting for transfers between devices, body(): lax.all_to_all(buffer, 'wide', split_axis=0, concat_axis=0, tiled=True)  74.6 us
    reduce_scatter x1, waiting for transfers between devices, body(): d_agg = lax.psum_scatter(d_part, 'narrow', scatter_dimension=0, tiled=True)  31.1 us
    all_to_all x1, starting transfers between devices, body(): lax.all_to_all(targets, 'wide', split_axis=0, concat_axis=0, tiled=True)  18.8 us
    another operation x3, other arithmetic  13.6 us
    scatter-add x1, other arithmetic, accumulate(): table.at[targets.reshape(-1)]  12.4 us
    all_to_all x1, starting transfers between devices, body(): lax.all_to_all(buffer, 'wide', split_axis=0, concat_axis=0, tiled=True)  11.1 us
  transfers between devices with their start and end apart: 5, of which 4 were waited for; matrix products, arithmetic and copies ran while one was open for 11% of the time, Pallas kernels for 0%

commit v1 on v0

v1 whole, which is shorter than its diff:
```python
import functools

import jax
import jax.numpy as jnp
from jax import lax
from jax.experimental import pallas as pl
from jax.experimental.pallas import tpu as pltpu
from jax.sharding import PartitionSpec as P

FAN = 25
NODES_DEV = 512
REL = 5
F = 768
HALF = 384
HID = 64
XN, ZN, YN = 4, 12, 8
GROUP = 16
RA = 3
PA, PB = RA * HALF, (REL - RA) * HALF
GCOLS = REL * F + 2 * F
GWIN = 512
MESH = pl.DeviceIdType.MESH
f32, bf16, i32 = jnp.float32, jnp.bfloat16, jnp.int32


def window_start(k):
    return 128 * ((7 * k) // 2)


def kernel(agg, wr, seeds, ws, kind, cot, cnt, key, tout, gout,
           wother, dp, dother, dsend, dbuf, kall, kf, c_ref, ma, mb,
           wx, wbx, wz, wbz, gz, gx, tsend, tbuf, tall,
           s_w, r_w, s_dp, r_dp, s_kx, r_kx, s_kz, r_kz, s_d, r_d, s_wx, r_wx, s_wz, r_wz,
           s_ax, r_ax, s_az, r_az, s_bx, r_bx, s_bz, r_bz, s_gz, r_gz, s_gx, r_gx,
           s_t, r_t, s_ta, r_ta, s_tc, r_tc):
    wide, narrow = lax.axis_index("wide"), lax.axis_index("narrow")
    x, z = wide // ZN, wide % ZN
    y, core = narrow // 2, narrow % 2
    other = 1 - core

    def at_x(p):
        return (p * ZN + z, narrow)

    def at_z(p):
        return (x * ZN + p, narrow)

    def at_y(p):
        return (wide, p * 2 + core)

    partner = (wide, y * 2 + other)

    def copy(src, dst, s, r, to):
        return pltpu.make_async_remote_copy(
            src_ref=src, dst_ref=dst, send_sem=s, recv_sem=r, device_id=to, device_id_type=MESH)

    barrier = pltpu.get_barrier_semaphore()

    def greet(to):
        pl.semaphore_signal(barrier, inc=1, device_id=to, device_id_type=MESH)

    def each(n, fn):
        def step(d, carry):
            fn(d)
            return carry
        lax.fori_loop(1, n, step, 0)

    each(XN, lambda d: greet(at_x((x + d) % XN)))
    each(ZN, lambda d: greet(at_z((z + d) % ZN)))
    each(YN, lambda d: greet(at_y((y + d) % YN)))
    greet(partner)
    pl.semaphore_wait(barrier, XN + ZN + YN - 2)

    def cp_w(r):
        cols = pl.ds(pl.multiple_of(r * F + other * HALF, 128), HALF)
        return copy(wr.at[:, cols], wother.at[:, pl.ds(r * HALF, HALF)], s_w.at[r], r_w.at[r], partner)

    def cp_kx(d):
        return copy(kall.at[z, x], kall.at[z, x], s_kx.at[d], r_kx.at[d], at_x((x + d) % XN))

    def cp_kz(d):
        return copy(kall.at[z], kall.at[z], s_kz.at[d], r_kz.at[d], at_z((z + d) % ZN))

    def cp_d(d):
        p = (y + d) % YN
        return copy(dsend.at[p], dbuf.at[y], s_d.at[d], r_d.at[d], at_y(p))

    def cp_wx(d):
        p = (x + d) % XN
        return copy(wx.at[p], wbx.at[x], s_wx.at[d], r_wx.at[d], at_x(p))

    def cp_wz(d):
        p = (z + d) % ZN
        return copy(wz.at[p], wbz.at[z], s_wz.at[d], r_wz.at[d], at_z(p))

    def cp_gz(d):
        return copy(gz.at[z], gz.at[z], s_gz.at[d], r_gz.at[d], at_z((z + d) % ZN))

    def cp_gx(d):
        return copy(gz, gx.at[x], s_gx.at[d], r_gx.at[d], at_x((x + d) % XN))

    def cp_t(d):
        p = (y + d) % YN
        return copy(tsend.at[p], tbuf.at[y], s_t.at[d], r_t.at[d], at_y(p))

    def cp_ta(d):
        return copy(tall.at[core, y], tall.at[core, y], s_ta.at[d], r_ta.at[d], at_y((y + d) % YN))

    def cp_tc(d):
        p = (y - d + YN) % YN
        return copy(tall.at[core, p], tall.at[core, p], s_tc.at[d], r_tc.at[d], partner)

    def cp_ax(d):
        return copy(ma.at[z, x], ma.at[z, x], s_ax.at[d], r_ax.at[d], at_x((x + d) % XN))

    def held(direction, t):
        return (z - (t - 1) + ZN) % ZN if direction == 0 else (z + (t - 1)) % ZN

    def next_z(direction):
        return at_z((z + 1) % ZN if direction == 0 else (z + ZN - 1) % ZN)

    def cp_az(direction, t, h):
        part = ma.at[held(direction, t), pl.ds(2 * h, 2)]
        i = (direction * 6 + t - 1) * 2 + h
        return copy(part, part, s_az.at[i], r_az.at[i], next_z(direction))

    def az_parts(t):
        return [(0, 0), (1, 0), (0, 1), (1, 1)] if t < 6 else [(0, 0), (1, 1)]

    def cp_bz(direction, t):
        cols = pl.ds(0, PB) if t < 6 else pl.ds(direction * (PB // 2), PB // 2)
        part = mb.at[held(direction, t), x, :, cols]
        i = direction * 6 + t - 1
        return copy(part, part, s_bz.at[i], r_bz.at[i], next_z(direction))

    def cp_bx(d, piece):
        if piece <= 5:
            p = (z - piece + ZN) % ZN
        elif piece <= 10:
            p = (z + piece - 5) % ZN
        else:
            p = (z + 6) % ZN
        part = mb.at[p, x]
        i = piece * XN + d
        return copy(part, part, s_bx.at[i], r_bx.at[i], at_x((x + d) % XN))

    def start(fn, n):
        each(n, lambda d: fn(d).start())

    def arrive(fn, n):
        each(n, lambda d: fn(d).wait_recv())

    for r in range(REL):
        cp_w(r).start()
    kall[z, x] = key[...]
    start(cp_kx, XN)

    contract = (((1,), (1,)), ((), ()))
    pre = lax.dot_general(wr[...], agg[...], contract, preferred_element_type=f32)
    zero = lax.dot_general(ws[0], seeds[...], contract, preferred_element_type=f32)
    one = lax.dot_general(ws[1], seeds[...], contract, preferred_element_type=f32)
    first = kind[...] == 0
    pre = pre + jnp.where(first, zero, one)
    sigma = 1.0 / (1.0 + jnp.exp(-pre))
    dpre = cot[...] * sigma * (1.0 + pre * (1.0 - sigma))
    dpre_b = dpre.astype(bf16)
    dp[...] = dpre_b
    cp_dp = copy(dp, dother, s_dp, r_dp, partner)
    cp_dp.start()

    for r in range(REL):
        g = jnp.dot(dpre_b, agg[:, r * F:(r + 1) * F], preferred_element_type=f32).astype(bf16)
        for p in range(XN):
            wx[p, :, r * F:(r + 1) * F] = g[p * 16:(p + 1) * 16]
    for t in range(2):
        mask = first if t == 0 else jnp.logical_not(first)
        part = jnp.where(mask, dpre_b.astype(f32), 0.0).astype(bf16)
        g = jnp.dot(part, seeds[...], preferred_element_type=f32).astype(bf16)
        for p in range(XN):
            wx[p, :, (REL + t) * F:(REL + t + 1) * F] = g[p * 16:(p + 1) * 16]

    mine = dpre_b.astype(f32).T.astype(bf16)
    cp_dp.wait_recv()
    theirs = dother[...].astype(f32).T.astype(bf16)
    for r in range(REL):
        cp_w(r).wait_recv()
        cols = pl.ds(pl.multiple_of(r * F + core * HALF, 128), HALF)
        d = jnp.dot(mine, wr[:, cols], preferred_element_type=f32)
        d = d + jnp.dot(theirs, wother[:, r * HALF:(r + 1) * HALF], preferred_element_type=f32)
        d = d.astype(bf16)
        for p in range(YN):
            dsend[p, :, r * HALF:(r + 1) * HALF] = d[p * GROUP:(p + 1) * GROUP]
    start(cp_d, YN)
    start(cp_wx, XN)

    arrive(cp_kx, XN)
    start(cp_kz, ZN)

    arrive(cp_wx, XN)
    for r in range(7):
        cols = slice(r * F, (r + 1) * F)
        total = wx[x, :, cols].astype(f32)
        for d in range(1, XN):
            total = total + wbx[(x + XN - d) % XN, :, cols].astype(f32)
        wx[x, :, cols] = total.astype(bf16)
    for k in range(ZN):
        wz[k] = wx[x, :, window_start(k):window_start(k) + GWIN]
    start(cp_wz, ZN)

    arrive(cp_d, YN)
    for r in range(REL):
        cols = slice(r * HALF, (r + 1) * HALF)
        total = dsend[y, :, cols].astype(f32)
        for d in range(1, YN):
            total = total + dbuf[(y + YN - d) % YN, :, cols].astype(f32)
        message = (total / cnt[:, r:r + 1]).astype(bf16)
        if r < RA:
            ma[z, x, :, cols] = message
        else:
            mb[z, x, :, (r - RA) * HALF:(r - RA + 1) * HALF] = message

    def send_b(t):
        for direction in range(2):
            cp_bz(direction, t).start()

    def take_b(t):
        for direction in range(2):
            cp_bz(direction, t).wait_recv()
        if t < 6:
            send_b(t + 1)
            start(lambda d: cp_bx(d, t), XN)
            start(lambda d: cp_bx(d, 5 + t), XN)
        else:
            start(lambda d: cp_bx(d, 11), XN)

    def send_a(t, part):
        cp_az(part[0], t, part[1]).start()

    def take_a(t):
        for part in az_parts(t):
            cp_az(part[0], t, part[1]).wait_recv()
            if t < 6 and part in az_parts(t + 1):
                send_a(t + 1, part)

    send_b(1)
    start(cp_ax, XN)
    start(lambda d: cp_bx(d, 0), XN)

    arrive(cp_kz, ZN)
    base = (wide * NODES_DEV).astype(f32)
    keys = kall[...].reshape(XN * ZN * GROUP, 128).astype(f32).T
    for hh in range(2):
        v = keys - (base + 256.0 * hh)
        kf[hh] = jnp.where((v >= 0.0) & (v < 256.0), v, -1.0)

    def build(r, part):
        rows = lax.broadcasted_iota(i32, (256, 128), 0).astype(f32).astype(bf16)

        def tile(i, carry):
            hh = i // 6
            cols = pl.ds(pl.multiple_of((i % 6) * 128, 128), 128)
            acc = jnp.zeros((256, 128), bf16)
            for f in range(FAN):
                row = kf[hh, r * FAN + f:r * FAN + f + 1, cols]
                named = jnp.broadcast_to(row, (16, 128)).astype(bf16)
                named = jnp.concatenate([named] * 16, axis=0)
                acc = acc + jnp.where(rows == named, jnp.ones((), bf16), jnp.zeros((), bf16))
            c_ref[r, pl.ds(pl.multiple_of(hh * 256, 256), 256), cols] = acc
            return carry

        lax.fori_loop(part * 6, part * 6 + 6, tile, 0)

    take_b(1)
    arrive(cp_ax, XN)
    for part in az_parts(1):
        send_a(1, part)
    for t in range(1, 6):
        take_b(t + 1)
        build(t - 1, 0)
        take_a(t)
        build(t - 1, 1)

    arrive(cp_wz, ZN)
    total = wz[z].astype(f32)
    for d in range(1, ZN):
        total = total + wbz[(z + ZN - d) % ZN].astype(f32)
    gz[z] = total.astype(bf16)

    for piece in range(12):
        arrive(lambda d: cp_bx(d, piece), XN)

    def times(r):
        if r < RA:
            m = ma[:, :, :, r * HALF:(r + 1) * HALF]
        else:
            m = mb[:, :, :, (r - RA) * HALF:(r - RA + 1) * HALF]
        return jnp.dot(c_ref[r], m.reshape(XN * ZN * GROUP, HALF), preferred_element_type=f32)

    table = times(3) + times(4)
    take_a(6)
    start(cp_gz, ZN)
    table = table + times(0) + times(1) + times(2)
    for p in range(YN):
        tsend[p] = table[p * 64:(p + 1) * 64].astype(bf16)
    start(cp_t, YN)
    arrive(cp_gz, ZN)
    start(cp_gx, XN)
    arrive(cp_t, YN)
    total = tsend[y].astype(f32)
    for d in range(1, YN):
        total = total + tbuf[(y + YN - d) % YN].astype(f32)
    tall[core, y] = total.astype(bf16)
    start(cp_ta, YN)
    cp_tc(0).start()

    arrive(cp_gx, XN)
    gx[x] = gz[...]
    for p in range(XN):
        for k in range(ZN):
            gout[p * 16:(p + 1) * 16, window_start(k):window_start(k) + GWIN] = gx[p, k]

    def hand_on(d):
        cp_ta(d).wait_recv()
        cp_tc(d).start()

    each(YN, hand_on)
    cp_tc_wait = lambda d: copy(tall.at[other, (y - d + YN) % YN], tall.at[other, (y - d + YN) % YN],
                                s_tc.at[d], r_tc.at[d], partner).wait_recv()
    lax.fori_loop(0, YN, lambda d, carry: (cp_tc_wait(d), carry)[1], 0)
    for c in range(2):
        for p in range(YN):
            tout[p * 64:(p + 1) * 64, c * HALF:(c + 1) * HALF] = tall[c, p]

    def sent(fn, n):
        each(n, lambda d: fn(d).wait_send())

    for r in range(REL):
        cp_w(r).wait_send()
    cp_dp.wait_send()
    sent(cp_kx, XN)
    sent(cp_kz, ZN)
    sent(cp_d, YN)
    sent(cp_wx, XN)
    sent(cp_wz, ZN)
    sent(cp_ax, XN)
    sent(cp_gz, ZN)
    sent(cp_gx, XN)
    sent(cp_t, YN)
    sent(cp_ta, YN)
    lax.fori_loop(0, YN, lambda d, carry: (cp_tc(d).wait_send(), carry)[1], 0)
    for piece in range(12):
        sent(lambda d: cp_bx(d, piece), XN)
    for t in range(1, 7):
        for direction in range(2):
            cp_bz(direction, t).wait_send()
        for part in az_parts(t):
            cp_az(part[0], t, part[1]).wait_send()


def body(agg_rows, seed_feats, seed_type, w_rel, w_self, cotangent, counts, owner, local_row):
    y = lax.axis_index("narrow") // 2
    count = lax.dynamic_slice_in_dim(counts, y * GROUP, GROUP, 0)
    slots = GROUP * REL * FAN
    names = lax.dynamic_slice_in_dim(owner[:, 0], y * slots, slots, 0) * NODES_DEV
    names = names + lax.dynamic_slice_in_dim(local_row, y * slots, slots, 0)
    live = lax.broadcasted_iota(i32, (1, 1, FAN), 2) < count[:, :, None]
    key = jnp.where(live.reshape(GROUP, REL * FAN), names.reshape(GROUP, REL * FAN), -1)
    key = jnp.pad(key, ((0, 0), (0, 128 - REL * FAN)), constant_values=-1)
    cnt = jnp.pad(count.astype(f32), ((0, 0), (0, 128 - REL)), constant_values=1.0)
    vmem = pltpu.VMEM
    dma = lambda n: pltpu.SemaphoreType.DMA((n,))
    one = pltpu.SemaphoreType.DMA
    pairs = lambda *sizes: [dma(n) for n in sizes for _ in range(2)]
    table, grads = pl.pallas_call(
        kernel,
        out_shape=(jax.ShapeDtypeStruct((NODES_DEV, F), bf16), jax.ShapeDtypeStruct((HID, GCOLS), bf16)),
        in_specs=[pl.BlockSpec(memory_space=vmem)] * 8,
        out_specs=(pl.BlockSpec(memory_space=vmem),) * 2,
        scratch_shapes=[
            vmem((HID, REL * HALF), bf16),
            vmem((HID, 128), bf16),
            vmem((HID, 128), bf16),
            vmem((YN, GROUP, REL * HALF), bf16),
            vmem((YN, GROUP, REL * HALF), bf16),
            vmem((ZN, XN, GROUP, 128), i32),
            vmem((2, 128, XN * ZN * GROUP), f32),
            vmem((REL, NODES_DEV, XN * ZN * GROUP), bf16),
            vmem((ZN, XN, GROUP, PA), bf16),
            vmem((ZN, XN, GROUP, PB), bf16),
            vmem((XN, 16, GCOLS), bf16),
            vmem((XN, 16, GCOLS), bf16),
            vmem((ZN, 16, GWIN), bf16),
            vmem((ZN, 16, GWIN), bf16),
            vmem((ZN, 16, GWIN), bf16),
            vmem((XN, ZN, 16, GWIN), bf16),
            vmem((YN, 64, HALF), bf16),
            vmem((YN, 64, HALF), bf16),
            vmem((2, YN, 64, HALF), bf16),
            dma(REL), dma(REL), one, one,
            *pairs(XN, ZN, YN, XN, ZN, XN, 24, 48, 12, ZN, XN, YN, YN, YN),
        ],
        compiler_params=pltpu.CompilerParams(
            collective_id=0, has_side_effects=True, vmem_limit_bytes=56 * 1024 * 1024),
        cost_estimate=pl.CostEstimate(flops=3_500_000_000, bytes_accessed=8_000_000, transcendentals=8192),
    )(agg_rows, w_rel.T, seed_feats, w_self.transpose(0, 2, 1), seed_type.reshape(1, -1), cotangent.T, cnt, key)
    grad_rel = grads[:, :REL * F].astype(f32).T
    grad_self = jnp.stack([grads[:, (REL + t) * F:(REL + t + 1) * F].astype(f32).T for t in range(2)])
    return table.astype(f32), grad_rel, grad_self


def solution(mesh):
    in_specs = (
        P("wide", None),
        P("wide", None),
        P("wide"),
        P(None, "narrow"),
        P(None, None, "narrow"),
        P("wide", "narrow"),
        P("wide", None),
        P("wide", None),
        P("wide"),
    )
    out_specs = (P("wide", None), P(None, "narrow"), P(None, None, "narrow"))
    return jax.shard_map(body, mesh=mesh, in_specs=in_specs, out_specs=out_specs, check_vma=False)
```

time: 517 us -> 110 us (0.21)
  waiting for transfers between devices: 400 us -> 0 us
  Pallas kernels: 0 us -> 99.7 us
  other arithmetic: 40.6 us -> 5.82 us
  starting transfers between devices: 30.3 us -> 0 us
  local copies, waits for them, and re-layouts: 22.8 us -> 2.39 us
  between operations: 15.8 us -> 0.7 us
  matrix products: 7.22 us -> 0 us
    psum x2 -> x0, waiting for transfers between devices: 295 us -> none  [the longest x1 165 us: sum_weights(): return lax.psum((rel_local, self_local), 'wide')]
    pallas_call x0 -> x1, Pallas kernels: none -> 99.7 us  [body(): pl.pallas_call(kernel, out_shape=(jax.ShapeDtypeStruct((NODES_DEV, F), bf...]
    all_to_all x2 -> x0, waiting for transfers between devices: 74.6 us -> none  [the longest x1 74.6 us: body(): lax.all_to_all(buffer, 'wide', split_axis=0, concat_axis=0, tiled=True)]
    reduce_scatter x1 -> x0, waiting for transfers between devices: 31.1 us -> none  [body(): d_agg = lax.psum_scatter(d_part, 'narrow', scatter_dimension=0, tiled=True)]
    all_to_all x2 -> x0, starting transfers between devices: 30 us -> none  [the longest x1 18.8 us: body(): lax.all_to_all(targets, 'wide', split_axis=0, concat_axis=0, tiled=True)]
    another operation x4 -> x1, other arithmetic: 14.3 us -> 0.77 us  [body(): jnp.stack([grads[:, (REL + t) * F:(REL + t + 1) * F].astype(f32).T for t...]
    scatter-add x1 -> x0, other arithmetic: 12.4 us -> none  [accumulate(): table.at[targets.reshape(-1)]]
    scatter x1 -> x0, other arithmetic: 9.87 us -> none  [pack_slots(): buffer = jnp.zeros((total, width), jnp.bfloat16).at[places].set(values)]
  transfers between devices with their start and end apart: 5 -> 0, of which waited for: 4 -> 0; matrix products, arithmetic and copies ran while one was open for 11% -> 0% of each run, Pallas kernels for 0% -> 0%
where the time goes in v1:
time: 110 us; the launch traced here: 109 us
  Pallas kernels  99.7 us (91%)
  other arithmetic  5.82 us (5%)
  local copies, waits for them, and re-layouts  2.39 us (2%)
    pallas_call x1, Pallas kernels, body(): pl.pallas_call(kernel, out_shape=(jax.ShapeDtypeStruct((NODES_DEV, F), bf...  99.7 us
    convert_element_type x1, other arithmetic, body(): return (table.astype(f32), grad_rel, grad_self)  2.45 us

profile of v1, /device:TPU:1, one launch (start us, length us, event | category | flops | bytes accessed | tf_op | source)
XLA Modules:
  0.0 108.6 jit_solution(5386602129602574575)
XLA Ops:
  0.6 0.0 copy-start
  0.7 0.7 copy-done
  1.3 0.1 constant_dynamic-slice_fusion
  1.4 0.1 copy.14
  1.5 0.6 pad.8.cnt
  2.1 0.8 dynamic-slice_multiply_fusion
  2.9 0.8 dynamic-slice_add_fusion
  3.7 0.1 reshape.20
  3.8 0.1 lt.31
  3.8 0.1 lt.32
  3.9 0.1 lt.29
  4.0 0.6 pad.9.key
  4.6 99.7 %shard_map.112 = (bf16[512,768]{1,0:T(8,128)(2,1)}, bf16[64,5376]{1,0:T(8,128)(2,1)}) custom-call(bf16[128,3840]{1,0:T(8,128)(2,1)} %agg.1, bf16[64,3840]{1,0:T(8,128)(2,1)} %bitcast.16, bf16[128,768]{1,0:T(8,128)(2,1)} %seeds.1, bf16[2,64,768]{2,1,0:T(8,128)(2,1)} %bitcast.17, s32[1,128]{1,0:T(1,128)} %bitcast.19, f32[64,128]{1,0:T(8,128)} %bitcast.18, ...), custom_call_target="tpu_custom_call" | custom-call | flops 3500000000 | bytes 8000000 | tf_op jit(solution)/shard_map/pallas_call | solution.py:373
  104.3 0.0 copy-start.1
  104.3 2.5 %convert_element_type.10 = f32[512,768]{1,0:T(8,128)} convert(bf16[512,768]{1,0:T(8,128)(2,1)} %get-tuple-element.5) | non-fusion elementwise | flops 393216 | bytes 2359296 | tf_op jit(solution)/shard_map/convert_element_type | solution.py:407
  106.8 0.0 copy-done.1
  106.8 1.0 convert_bitcast_fusion
  107.8 0.8 maximum_convert_fusion
  (4 shorter events, 0.0 us)
Async XLA Ops:
  0.6 0.7 copy-start
  104.3 2.5 %copy-start.1 = (bf16[64,5376]{1,0:T(8,128)(2,1)S(1)}, bf16[64,5376]{1,0:T(8,128)(2,1)}, u32[]{:S(2)}) copy-start(bf16[64,5376]{1,0:T(8,128)(2,1)} %get-tuple-element.6) | copy-start | bytes 2064388

commit v2 on v1

v2 whole, which is shorter than its diff:
```python
import jax
import jax.numpy as jnp
from jax import lax
from jax.experimental import pallas as pl
from jax.experimental.pallas import tpu as pltpu
from jax.sharding import PartitionSpec as P

FAN = 25
NODES_DEV = 512
REL = 5
F = 768
HALF = 384
HID = 64
XN, ZN, YN = 4, 12, 8
GROUP = 16
ROWS = XN * ZN * GROUP
ALLH = 2 * YN * HID
SHARE = 256
PLAIN = REL * HALF - XN * SHARE
GCOLS = REL * F + 2 * F
GWIN = 512
DEAD = 32767
MESH = pl.DeviceIdType.MESH
f32, bf16, i32 = jnp.float32, jnp.bfloat16, jnp.int32


def window_start(k):
    return 128 * ((7 * k) // 2)


def kernel(agg, wr, seeds, ws, kind, cot, key, tout, gout,
           wnat, wy, wsh, dsend, dbuf, d_all, m_ref, inv, kall, kf, c_ref,
           wx, wbx, wz, wbz, gz, gx, tsend, tbuf, tall,
           s_w, r_w, s_kx, r_kx, s_kz, r_kz, s_kp, r_kp, s_d, r_d, s_wx, r_wx, s_wz, r_wz,
           s_wr, r_wr, s_sx, r_sx, s_dx, r_dx, s_px, r_px, s_d1, r_d1, s_dz, r_dz, s_pz, r_pz,
           s_gz, r_gz, s_gx, r_gx, s_t, r_t, s_ta, r_ta, s_tc, r_tc):
    wide, narrow = lax.axis_index("wide"), lax.axis_index("narrow")
    x, z = wide // ZN, wide % ZN
    y, core = narrow // 2, narrow % 2
    other = 1 - core

    def at_x(p):
        return (p * ZN + z, narrow)

    def at_z(p):
        return (x * ZN + p, narrow)

    def at_y(p):
        return (wide, p * 2 + core)

    partner = (wide, y * 2 + other)

    def at_xz(p, q):
        return (p * ZN + q, narrow)

    def copy(src, dst, s, r, to):
        return pltpu.make_async_remote_copy(
            src_ref=src, dst_ref=dst, send_sem=s, recv_sem=r, device_id=to, device_id_type=MESH)

    barrier = pltpu.get_barrier_semaphore()

    def greet(to):
        pl.semaphore_signal(barrier, inc=1, device_id=to, device_id_type=MESH)

    def each(n, fn, low=1):
        def step(d, carry):
            fn(d)
            return carry
        lax.fori_loop(low, n, step, 0)

    each(XN, lambda d: greet(at_x((x + d) % XN)))
    each(ZN, lambda d: greet(at_z((z + d) % ZN)))
    each(YN, lambda d: greet(at_y((y + d) % YN)))
    greet(partner)
    for step in (1, ZN - 1):
        each(XN, lambda d: greet(at_xz((x + d) % XN, (z + step) % ZN)))
    pl.semaphore_wait(barrier, 3 * XN + ZN + YN - 4)

    pending = []

    def start(fn, n):
        pending.append((fn, n))
        each(n, lambda d: fn(d).start())

    def start1(cp):
        pending.append((lambda d: cp, 2))
        cp.start()

    def arrive(fn, n):
        each(n, lambda d: fn(d).wait_recv())

    def cp_w(r):
        cols = pl.ds(pl.multiple_of(r * F + other * HALF, 128), HALF)
        return copy(wr.at[:, cols], wnat.at[core, :, pl.ds(r * HALF, HALF)], s_w.at[r], r_w.at[r], partner)

    def cp_kx(d):
        return copy(kall.at[z, x], kall.at[z, x], s_kx.at[d], r_kx.at[d], at_x((x + d) % XN))

    mine_x = pl.ds(2 * core, 2)

    def cp_kz(d):
        part = kall.at[z, mine_x]
        return copy(part, part, s_kz.at[d], r_kz.at[d], at_z((z + d) % ZN))

    def cp_kp(d):
        part = kall.at[(z - d + ZN) % ZN, mine_x]
        return copy(part, part, s_kp.at[d], r_kp.at[d], partner)

    def cp_d(d):
        p = (y + d) % YN
        return copy(dsend.at[p], dbuf.at[y], s_d.at[d], r_d.at[d], at_y(p))

    def cp_wx(d):
        p = (x + d) % XN
        return copy(wx.at[p], wbx.at[x], s_wx.at[d], r_wx.at[d], at_x(p))

    def cp_wz(d):
        p = (z + d) % ZN
        return copy(wz.at[p], wbz.at[z], s_wz.at[d], r_wz.at[d], at_z(p))

    def cp_gz(d):
        return copy(gz.at[z], gz.at[z], s_gz.at[d], r_gz.at[d], at_z((z + d) % ZN))

    def cp_gx(d):
        return copy(gz, gx.at[x], s_gx.at[d], r_gx.at[d], at_x((x + d) % XN))

    def cp_t(d):
        p = (y + d) % YN
        return copy(tsend.at[p], tbuf.at[y], s_t.at[d], r_t.at[d], at_y(p))

    def cp_tc(d, c=None):
        part = tall.at[core if c is None else c, (y - d + YN) % YN]
        return copy(part, part, s_tc.at[d], r_tc.at[d], partner)

    def held_y(direction, t):
        return (y - (t - 1) + YN) % YN if direction == 0 else (y + (t - 1)) % YN

    def next_y(direction):
        return at_y((y + 1) % YN if direction == 0 else (y + YN - 1) % YN)

    def cp_wr(direction, t, j):
        p, c = held_y(direction, t), core if j % 2 == 0 else other
        part = wy.at[c, p] if j < 2 else wsh.at[x, c, p]
        i = (direction * 4 + t - 1) * 4 + j
        return copy(part, part, s_wr.at[i], r_wr.at[i], next_y(direction))

    def send_w(t, j):
        for direction in range(2):
            if t < 4 or j % 2 == direction:
                start1(cp_wr(direction, t, j))

    def take_w(t, j):
        for direction in range(2):
            if t == 4 and j % 2 != direction:
                continue
            cp_wr(direction, t, j).wait_recv()
            if t < 3 or (t == 3 and j % 2 == direction):
                start1(cp_wr(direction, t + 1, j))
            if j == 3 and t < 4:
                start(lambda d, piece=direction * 3 + t - 1: cp_sx(d, piece), XN)
            if j == 3 and t == 4:
                start(lambda d: cp_sx(d, 6), XN)

    def take_all(t):
        for j in (2, 0, 3, 1):
            take_w(t, j)

    def cp_ta(d):
        return copy(tall.at[core, y], tall.at[core, y], s_ta.at[d], r_ta.at[d], at_y((y + d) % YN))

    def piece_y(piece):
        return (y - piece - 1 + YN) % YN if piece < 3 else (y + piece - 2) % YN if piece < 6 else (y + 4) % YN

    def cp_sx(d, piece):
        part = wsh.at[x, :, piece_y(piece)]
        i = piece * XN + d
        return copy(part, part, s_sx.at[i], r_sx.at[i], at_x((x + d) % XN))

    half = pl.ds(pl.multiple_of(core * (ALLH // 2), 128), ALLH // 2)

    def cp_dx(d):
        part = d_all.at[z, x, :, half]
        return copy(part, part, s_dx.at[d], r_dx.at[d], at_x((x + d) % XN))

    def cp_px(d):
        part = d_all.at[z, (x - d + XN) % XN, :, half]
        return copy(part, part, s_px.at[d], r_px.at[d], partner)

    def held(direction, t):
        return (z - (t - 1) + ZN) % ZN if direction == 0 else (z + (t - 1)) % ZN

    def next_z(direction):
        return at_z((z + 1) % ZN if direction == 0 else (z + ZN - 1) % ZN)

    def cp_dz(direction, t, h):
        part = d_all.at[held(direction, t), pl.ds(2 * h, 2), :, half]
        i = (direction * 6 + t - 1) * 2 + h
        return copy(part, part, s_dz.at[i], r_dz.at[i], next_z(direction))

    def cp_pz(direction, t):
        p = (z - t + ZN) % ZN if direction == 0 else (z + t) % ZN
        part = d_all.at[p, :, :, half]
        i = direction * 6 + t - 1
        return copy(part, part, s_pz.at[i], r_pz.at[i], partner)

    def cp_d1(direction, d):
        part = d_all.at[z, x, :, half]
        i = direction * XN + d
        to = at_xz((x + d) % XN, (z + 1) % ZN if direction == 0 else (z + ZN - 1) % ZN)
        return copy(part, part, s_d1.at[i], r_d1.at[i], to)

    def dz_parts(t):
        return [(0, 0), (1, 0), (0, 1), (1, 1)] if t < 6 else [(0, 0), (1, 1)]

    for r in range(REL):
        start1(cp_w(r))
    kall[z, x] = jnp.full((8, 128), DEAD * 65537, i32)
    kall[z, x, :, 0:REL * FAN] = key[...]
    start(cp_kx, XN)

    contract = (((1,), (1,)), ((), ()))
    zero = lax.dot_general(ws[0], seeds[...], contract, preferred_element_type=f32)
    one = lax.dot_general(ws[1], seeds[...], contract, preferred_element_type=f32)
    first = kind[...] == 0
    pre = jnp.where(first, zero, one)
    pre = pre + lax.dot_general(wr[...], agg[...], contract, preferred_element_type=f32)
    sigma = 1.0 / (1.0 + jnp.exp(-pre))
    dpre_b = (cot[...] * sigma * (1.0 + pre * (1.0 - sigma))).astype(bf16)

    wide_rows = jnp.concatenate([dpre_b.astype(f32), jnp.zeros((128 - HID, 128), f32)], axis=0)
    wide_rows = wide_rows.T.astype(bf16)
    for p in range(YN):
        dsend[p] = wide_rows[p * GROUP:(p + 1) * GROUP]
    start(cp_d, YN)
    dbuf[y] = dsend[y]

    def place_w(c):
        wy[c, y] = wnat[c, :, 0:PLAIN]
        for p in range(XN):
            wsh[p, c, y] = wnat[c, :, PLAIN + p * SHARE:PLAIN + (p + 1) * SHARE]

    for r in range(REL):
        cols = pl.ds(pl.multiple_of(r * F + core * HALF, 128), HALF)
        wnat[core, :, r * HALF:(r + 1) * HALF] = wr[:, cols]
    place_w(core)
    send_w(1, 2)
    send_w(1, 0)
    for r in range(REL):
        cp_w(r).wait_recv()
    place_w(other)
    send_w(1, 3)
    send_w(1, 1)
    arrive(cp_kx, XN)
    start(cp_kz, ZN)

    def grads(low, high):
        for r in range(low, high):
            if r < REL:
                g = jnp.dot(dpre_b, agg[:, r * F:(r + 1) * F], preferred_element_type=f32)
            else:
                mask = first if r == REL else jnp.logical_not(first)
                part = jnp.where(mask, dpre_b.astype(f32), 0.0).astype(bf16)
                g = jnp.dot(part, seeds[...], preferred_element_type=f32)
            g = g.astype(bf16)
            for p in range(XN):
                wx[p, :, r * F:(r + 1) * F] = g[p * 16:(p + 1) * 16]

    grads(0, 5)
    arrive(cp_d, YN)
    block = jnp.concatenate([dbuf[2 * p][:, 0:HID].astype(f32) if c == 0 else dbuf[2 * p + 1][:, 0:HID].astype(f32)
                             for p in range(YN // 2) for c in range(2)], axis=1).astype(bf16)
    d_all[z, x, :, half] = block
    for direction in range(2):
        pending.append((lambda d, direction=direction: cp_d1(direction, d - 1), XN + 1))
        each(XN, lambda d: cp_d1(direction, d).start(), 0)
    start(cp_dx, XN)
    grads(5, 7)
    pending.append((lambda d: cp_px(d - 1), XN + 1))
    cp_px(0).start()
    take_w(1, 2)

    def take_d(t):
        if t == 1:
            for direction in range(2):
                each(XN, lambda d: cp_d1(direction, d).wait_recv(), 0)
                for h in range(2):
                    start1(cp_dz(direction, 2, h))
                start1(cp_pz(direction, 1))
            return
        for part in dz_parts(t):
            cp_dz(part[0], t, part[1]).wait_recv()
            if t < 6 and part in dz_parts(t + 1):
                start1(cp_dz(part[0], t + 1, part[1]))
            if t < 6 and part[1] == 1:
                start1(cp_pz(part[0], t))
        if t == 6:
            start1(cp_pz(0, 6))

    def build(r):
        rows = lax.broadcasted_iota(i32, (256, 128), 0).astype(f32).astype(bf16)

        def tile(i, carry):
            hh = i // 6
            cols = pl.ds(pl.multiple_of((i % 6) * 128, 128), 128)
            acc = jnp.zeros((256, 128), bf16)
            for f in range(FAN):
                row = kf[hh, r * FAN + f:r * FAN + f + 1, cols]
                named = jnp.broadcast_to(row, (16, 128)).astype(bf16)
                named = jnp.concatenate([named] * 16, axis=0)
                acc = acc + jnp.where(rows == named, jnp.ones((), bf16), jnp.zeros((), bf16))
            c_ref[r, pl.ds(pl.multiple_of(hh * 256, 256), 256), cols] = acc
            return carry

        lax.fori_loop(0, 12, tile, 0)

    def hand_keys():
        pending.append((cp_kp, ZN))

        def hand(d):
            cp_kz(d).wait_recv()
            cp_kp(d).start()

        each(ZN, hand)

    def read_keys():
        arrive(cp_kp, ZN)
        packed = kall[...]
        keys = jnp.concatenate([packed % 65536, packed // 65536], axis=2).reshape(ROWS, 128)
        lane = lax.broadcasted_iota(i32, (ROWS, 128), 1)
        live = keys != DEAD
        for r in range(REL):
            mine = jnp.logical_and(live, jnp.logical_and(lane >= r * FAN, lane < (r + 1) * FAN))
            count = jnp.sum(jnp.where(mine, 1.0, 0.0), axis=1, keepdims=True)
            inv[r] = jnp.broadcast_to(1.0 / count, (ROWS, 128))
        keys = keys.astype(f32).T
        base = (wide * NODES_DEV).astype(f32)
        for hh in range(2):
            v = keys - (base + 256.0 * hh)
            kf[hh] = jnp.where((v >= 0.0) & (v < 256.0), v, -1.0)

    def sum_x():
        arrive(cp_wx, XN)
        for r in range(7):
            cols = slice(r * F, (r + 1) * F)
            total = wx[x, :, cols].astype(f32)
            for d in range(1, XN):
                total = total + wbx[(x + XN - d) % XN, :, cols].astype(f32)
            wx[x, :, cols] = total.astype(bf16)
        for k in range(ZN):
            wz[k] = wx[x, :, window_start(k):window_start(k) + GWIN]
        start(cp_wz, ZN)

    def multiply(cols, weights):
        out = jnp.dot(d_all[...].reshape(ROWS, ALLH), weights, preferred_element_type=f32)
        for low in range(cols.start, cols.stop, 128):
            m_ref[:, low:low + 128] = (out[:, low - cols.start:low - cols.start + 128] * inv[low // HALF]).astype(bf16)

    def shares(pieces):
        for piece in pieces:
            arrive(lambda d: cp_sx(d, piece), XN)

    hand_keys()
    take_w(1, 0)
    take_d(1)
    arrive(cp_dx, XN)
    each(XN, lambda d: cp_px(d).start())
    take_w(1, 3)
    take_w(1, 1)
    read_keys()
    take_d(2)
    build(0)
    take_d(3)
    take_w(2, 2)
    take_w(2, 0)
    build(1)
    take_d(4)
    take_w(2, 3)
    take_w(2, 1)
    build(2)
    take_d(5)
    start(cp_wx, XN)
    build(3)
    take_d(6)
    take_w(3, 2)
    take_w(3, 0)
    take_w(3, 3)
    take_w(3, 1)
    build(4)
    each(XN, lambda d: cp_px(d).wait_recv(), 0)
    for t in range(1, 6):
        for direction in range(2):
            cp_pz(direction, t).wait_recv()
    cp_pz(0, 6).wait_recv()
    take_w(4, 2)
    take_w(4, 3)
    take_w(4, 0)
    take_w(4, 1)
    sum_x()
    multiply(slice(0, 512), wy[:, :, :, 0:512].reshape(ALLH, 512))
    multiply(slice(512, PLAIN), wy[:, :, :, 512:PLAIN].reshape(ALLH, PLAIN - 512))
    shares(range(7))
    for p in range(XN):
        low = PLAIN + p * SHARE
        multiply(slice(low, low + SHARE), wsh[p].reshape(ALLH, SHARE))

    table = None
    for r in range(REL):
        out = jnp.dot(c_ref[r], m_ref[:, r * HALF:(r + 1) * HALF], preferred_element_type=f32)
        table = out if table is None else table + out
    for p in range(YN):
        tsend[p] = table[p * 64:(p + 1) * 64].astype(bf16)
    start(cp_t, YN)

    arrive(cp_wz, ZN)
    total = wz[z].astype(f32)
    for d in range(1, ZN):
        total = total + wbz[(z + ZN - d) % ZN].astype(f32)
    gz[z] = total.astype(bf16)
    start(cp_gz, ZN)

    arrive(cp_t, YN)
    total = tsend[y].astype(f32)
    for d in range(1, YN):
        total = total + tbuf[(y + YN - d) % YN].astype(f32)
    tall[core, y] = total.astype(bf16)
    start(cp_ta, YN)
    start1(cp_tc(0))
    arrive(cp_gz, ZN)
    start(cp_gx, XN)

    def hand_on(d):
        cp_ta(d).wait_recv()
        cp_tc(d).start()

    each(YN, hand_on)
    pending.append((cp_tc, YN))
    arrive(cp_gx, XN)
    gx[x] = gz[...]
    for p in range(XN):
        for k in range(ZN):
            gout[p * 16:(p + 1) * 16, window_start(k):window_start(k) + GWIN] = gx[p, k]

    each(YN, lambda d: cp_tc(d, other).wait_recv(), 0)
    for c in range(2):
        for p in range(YN):
            tout[p * 64:(p + 1) * 64, c * HALF:(c + 1) * HALF] = tall[c, p]

    for fn, n in pending:
        each(n, lambda d: fn(d).wait_send())


def body(agg_rows, seed_feats, seed_type, w_rel, w_self, cotangent, counts, owner, local_row):
    y = lax.axis_index("narrow") // 2
    count = lax.dynamic_slice_in_dim(counts, y * GROUP, GROUP, 0)
    slots = GROUP * REL * FAN
    names = lax.dynamic_slice_in_dim(owner[:, 0] * NODES_DEV + local_row, y * slots, slots, 0)
    live = lax.broadcasted_iota(i32, (1, 1, FAN), 2) < count[:, :, None]
    key = jnp.where(live.reshape(GROUP, REL * FAN), names.reshape(GROUP, REL * FAN), DEAD)
    key = key[:8] + key[8:] * 65536
    vmem = pltpu.VMEM
    dma = lambda n: pltpu.SemaphoreType.DMA((n,))
    pairs = lambda *sizes: [dma(n) for n in sizes for _ in range(2)]
    table, grads = pl.pallas_call(
        kernel,
        out_shape=(jax.ShapeDtypeStruct((NODES_DEV, F), bf16), jax.ShapeDtypeStruct((HID, GCOLS), bf16)),
        in_specs=[pl.BlockSpec(memory_space=vmem)] * 7,
        out_specs=(pl.BlockSpec(memory_space=vmem),) * 2,
        scratch_shapes=[
            vmem((2, HID, REL * HALF), bf16),
            vmem((2, YN, HID, PLAIN), bf16),
            vmem((XN, 2, YN, HID, SHARE), bf16),
            vmem((YN, GROUP, 128), bf16),
            vmem((YN, GROUP, 128), bf16),
            vmem((ZN, XN, GROUP, ALLH), bf16),
            vmem((ROWS, REL * HALF), bf16),
            vmem((REL, ROWS, 128), f32),
            vmem((ZN, XN, 8, 128), i32),
            vmem((2, 128, ROWS), f32),
            vmem((REL, NODES_DEV, ROWS), bf16),
            vmem((XN, 16, GCOLS), bf16),
            vmem((XN, 16, GCOLS), bf16),
            vmem((ZN, 16, GWIN), bf16),
            vmem((ZN, 16, GWIN), bf16),
            vmem((ZN, 16, GWIN), bf16),
            vmem((XN, ZN, 16, GWIN), bf16),
            vmem((YN, 64, HALF), bf16),
            vmem((YN, 64, HALF), bf16),
            vmem((2, YN, 64, HALF), bf16),
            *pairs(REL, XN, ZN, ZN, YN, XN, ZN, 32, 28, XN, XN, 8, 24, 12, ZN, XN, YN, YN, YN),
        ],
        compiler_params=pltpu.CompilerParams(
            collective_id=0, has_side_effects=True, vmem_limit_bytes=56 * 1024 * 1024),
        cost_estimate=pl.CostEstimate(flops=6_500_000_000, bytes_accessed=8_000_000, transcendentals=8192),
    )(agg_rows, w_rel.T, seed_feats, w_self.transpose(0, 2, 1), seed_type.reshape(1, -1), cotangent.T, key)
    grad_rel = grads[:, :REL * F].astype(f32).T
    grad_self = jnp.stack([grads[:, (REL + t) * F:(REL + t + 1) * F].astype(f32).T for t in range(2)])
    return table.astype(f32), grad_rel, grad_self


def solution(mesh):
    in_specs = (
        P("wide", None),
        P("wide", None),
        P("wide"),
        P(None, "narrow"),
        P(None, None, "narrow"),
        P("wide", "narrow"),
        P("wide", None),
        P("wide", None),
        P("wide"),
    )
    out_specs = (P("wide", None), P(None, "narrow"), P(None, None, "narrow"))
    return jax.shard_map(body, mesh=mesh, in_specs=in_specs, out_specs=out_specs, check_vma=False)
```

time: 110 us -> 102 us (0.927)
  Pallas kernels: 99.7 us -> 93.6 us
  local copies, waits for them, and re-layouts: 2.39 us -> 0.52 us
    pallas_call x1, Pallas kernels: 99.7 us -> 93.6 us  [body(): pl.pallas_call(kernel, out_shape=(jax.ShapeDtypeStruct((NODES_DEV, F), bf...]
    pad x2 -> x0, local copies, waits for them, and re-layouts: 1.22 us -> none  [the longest x1 0.61 us: body(): key = jnp.pad(key, ((0, 0), (0, 128 - REL * FAN)), constant_values=-1)]
where the time goes in v2:
time: 102 us
  Pallas kernels  93.6 us (92%)
  other arithmetic  6.67 us (7%)
    pallas_call x1, Pallas kernels, body(): pl.pallas_call(kernel, out_shape=(jax.ShapeDtypeStruct((NODES_DEV, F), bf...  93.6 us
    convert_element_type x1, other arithmetic, body(): return (table.astype(f32), grad_rel, grad_self)  2.45 us

profile of v2, /device:TPU:1, one launch (start us, length us, event | category | flops | bytes accessed | tf_op | source)
XLA Modules:
  0.0 101.5 jit_solution(10466337240312042907)
XLA Ops:
  0.6 0.0 copy-start
  0.7 1.0 %multiply_reduce_fusion = s32[16000]{0:T(1024)S(1)} fusion(s32[16000,1]{0,1:T(1,128)} %param.16), kind=kLoop, calls=%fused_computation.4 | loop fusion | flops 16000 | bytes 128000 | tf_op jit(solution)/shard_map/mul | solution.py:456
  1.7 0.8 dynamic-slice_add_fusion
  2.5 0.1 reshape.19
  2.6 0.0 copy-done
  2.6 0.1 constant_dynamic-slice_fusion
  2.7 0.1 copy.13
  2.8 0.1 lt.30
  2.8 0.1 lt.31
  2.9 0.1 lt.27
  3.0 0.6 fusion.key
  3.6 93.6 %shard_map.112 = (bf16[512,768]{1,0:T(8,128)(2,1)}, bf16[64,5376]{1,0:T(8,128)(2,1)}) custom-call(bf16[128,3840]{1,0:T(8,128)(2,1)} %agg.1, bf16[64,3840]{1,0:T(8,128)(2,1)} %bitcast.14, bf16[128,768]{1,0:T(8,128)(2,1)} %seeds.1, bf16[2,64,768]{2,1,0:T(8,128)(2,1)} %bitcast.15, s32[1,128]{1,0:T(1,128)} %bitcast.17, f32[64,128]{1,0:T(8,128)} %bitcast.16, ...), custom_call_target="tpu_custom_call" | custom-call | flops 6499999744 | bytes 8000000 | tf_op jit(solution)/shard_map/pallas_call | solution.py:463
  97.3 0.0 copy-start.1
  97.3 2.5 %convert_element_type.2 = f32[512,768]{1,0:T(8,128)} convert(bf16[512,768]{1,0:T(8,128)(2,1)} %get-tuple-element.5) | non-fusion elementwise | flops 393216 | bytes 2359296 | tf_op jit(solution)/shard_map/convert_element_type | solution.py:497
  99.7 0.0 copy-done.1
  99.7 1.0 convert_bitcast_fusion
  100.8 0.8 maximum_convert_fusion
  (3 shorter events, 0.0 us)
Async XLA Ops:
  0.6 2.0 %copy-start = (s32[128,5]{0,1:T(8,128)S(1)}, s32[128,5]{0,1:T(8,128)}, u32[]{:S(2)}) copy-start(s32[128,5]{0,1:T(8,128)} %param.15) | copy-start | bytes 7684
  97.3 2.5 %copy-start.1 = (bf16[64,5376]{1,0:T(8,128)(2,1)S(1)}, bf16[64,5376]{1,0:T(8,128)(2,1)}, u32[]{:S(2)}) copy-start(bf16[64,5376]{1,0:T(8,128)(2,1)} %get-tuple-element.6) | copy-start | bytes 2064388

commit v3 on v2

--- a/solution.py
+++ b/solution.py
@@ -124,13 +124,18 @@
     def cp_gx(d):
         return copy(gz, gx.at[x], s_gx.at[d], r_gx.at[d], at_x((x + d) % XN))
 
-    def cp_t(d):
+    def part_rows(h):
+        return pl.ds(32 * h, 32)
+
+    def cp_t(d, h):
         p = (y + d) % YN
-        return copy(tsend.at[p], tbuf.at[y], s_t.at[d], r_t.at[d], at_y(p))
-
-    def cp_tc(d, c=None):
-        part = tall.at[core if c is None else c, (y - d + YN) % YN]
-        return copy(part, part, s_tc.at[d], r_tc.at[d], partner)
+        i = h * YN + d
+        return copy(tsend.at[p, part_rows(h)], tbuf.at[y, part_rows(h)], s_t.at[i], r_t.at[i], at_y(p))
+
+    def cp_tc(d, h, c=None):
+        part = tall.at[core if c is None else c, (y - d + YN) % YN, part_rows(h)]
+        i = h * YN + d
+        return copy(part, part, s_tc.at[i], r_tc.at[i], partner)
 
     def held_y(direction, t):
         return (y - (t - 1) + YN) % YN if direction == 0 else (y + (t - 1)) % YN
@@ -165,8 +170,10 @@
         for j in (2, 0, 3, 1):
             take_w(t, j)
 
-    def cp_ta(d):
-        return copy(tall.at[core, y], tall.at[core, y], s_ta.at[d], r_ta.at[d], at_y((y + d) % YN))
+    def cp_ta(d, h):
+        part = tall.at[core, y, part_rows(h)]
+        i = h * YN + d
+        return copy(part, part, s_ta.at[i], r_ta.at[i], at_y((y + d) % YN))
 
     def piece_y(piece):
         return (y - piece - 1 + YN) % YN if piece < 3 else (y + piece - 2) % YN if piece < 6 else (y + 4) % YN
@@ -385,14 +392,14 @@
     take_w(3, 0)
     take_w(3, 3)
     take_w(3, 1)
+    take_w(4, 2)
+    take_w(4, 3)
     build(4)
     each(XN, lambda d: cp_px(d).wait_recv(), 0)
     for t in range(1, 6):
         for direction in range(2):
             cp_pz(direction, t).wait_recv()
     cp_pz(0, 6).wait_recv()
-    take_w(4, 2)
-    take_w(4, 3)
     take_w(4, 0)
     take_w(4, 1)
     sum_x()
@@ -409,7 +416,8 @@
         table = out if table is None else table + out
     for p in range(YN):
         tsend[p] = table[p * 64:(p + 1) * 64].astype(bf16)
-    start(cp_t, YN)
+    for h in range(2):
+        start(lambda d, h=h: cp_t(d, h), YN)
 
     arrive(cp_wz, ZN)
     total = wz[z].astype(f32)
@@ -418,29 +426,33 @@
     gz[z] = total.astype(bf16)
     start(cp_gz, ZN)
 
-    arrive(cp_t, YN)
-    total = tsend[y].astype(f32)
-    for d in range(1, YN):
-        total = total + tbuf[(y + YN - d) % YN].astype(f32)
-    tall[core, y] = total.astype(bf16)
-    start(cp_ta, YN)
-    start1(cp_tc(0))
+    for h in range(2):
+        arrive(lambda d: cp_t(d, h), YN)
+        rows = slice(32 * h, 32 * h + 32)
+        total = tsend[y, rows].astype(f32)
+        for d in range(1, YN):
+            total = total + tbuf[(y + YN - d) % YN, rows].astype(f32)
+        tall[core, y, rows] = total.astype(bf16)
+        start(lambda d, h=h: cp_ta(d, h), YN)
+        start1(cp_tc(0, h))
     arrive(cp_gz, ZN)
     start(cp_gx, XN)
 
-    def hand_on(d):
-        cp_ta(d).wait_recv()
-        cp_tc(d).start()
-
-    each(YN, hand_on)
-    pending.append((cp_tc, YN))
+    for h in range(2):
+        def hand_on(d):
+            cp_ta(d, h).wait_recv()
+            cp_tc(d, h).start()
+
+        each(YN, hand_on)
+        pending.append((lambda d, h=h: cp_tc(d, h), YN))
     arrive(cp_gx, XN)
     gx[x] = gz[...]
     for p in range(XN):
         for k in range(ZN):
             gout[p * 16:(p + 1) * 16, window_start(k):window_start(k) + GWIN] = gx[p, k]
 
-    each(YN, lambda d: cp_tc(d, other).wait_recv(), 0)
+    for h in range(2):
+        each(YN, lambda d: cp_tc(d, h, other).wait_recv(), 0)
     for c in range(2):
         for p in range(YN):
             tout[p * 64:(p + 1) * 64, c * HALF:(c + 1) * HALF] = tall[c, p]
@@ -486,7 +498,7 @@
             vmem((YN, 64, HALF), bf16),
             vmem((YN, 64, HALF), bf16),
             vmem((2, YN, 64, HALF), bf16),
-            *pairs(REL, XN, ZN, ZN, YN, XN, ZN, 32, 28, XN, XN, 8, 24, 12, ZN, XN, YN, YN, YN),
+            *pairs(REL, XN, ZN, ZN, YN, XN, ZN, 32, 28, XN, XN, 8, 24, 12, ZN, XN, 16, 16, 16),
         ],
         compiler_params=pltpu.CompilerParams(
             collective_id=0, has_side_effects=True, vmem_limit_bytes=56 * 1024 * 1024),

time: 102 us -> 102 us (level)
  no operation moved by 1% of the time
where the time goes in v3:
time: 102 us; the launch traced here: 101 us
  Pallas kernels  92.8 us (91%)
  other arithmetic  6.67 us (7%)
    pallas_call x1, Pallas kernels, body(): pl.pallas_call(kernel, out_shape=(jax.ShapeDtypeStruct((NODES_DEV, F), bf...  92.8 us
    convert_element_type x1, other arithmetic, body(): return (table.astype(f32), grad_rel, grad_self)  2.45 us

profile of v3, /device:TPU:1, one launch (start us, length us, event | category | flops | bytes accessed | tf_op | source)
XLA Modules:
  0.0 100.7 jit_solution(3409387370146141680)
XLA Ops:
  0.6 0.0 copy-start
  0.7 1.0 %multiply_reduce_fusion = s32[16000]{0:T(1024)S(1)} fusion(s32[16000,1]{0,1:T(1,128)} %param.16), kind=kLoop, calls=%fused_computation.4 | loop fusion | flops 16000 | bytes 128000 | tf_op jit(solution)/shard_map/mul | solution.py:468
  1.7 0.8 dynamic-slice_add_fusion
  2.5 0.1 reshape.19
  2.6 0.0 copy-done
  2.6 0.1 constant_dynamic-slice_fusion
  2.7 0.1 copy.13
  2.8 0.1 lt.30
  2.8 0.1 lt.31
  2.9 0.1 lt.27
  3.0 0.6 fusion.key
  3.6 92.8 %shard_map.112 = (bf16[512,768]{1,0:T(8,128)(2,1)}, bf16[64,5376]{1,0:T(8,128)(2,1)}) custom-call(bf16[128,3840]{1,0:T(8,128)(2,1)} %agg.1, bf16[64,3840]{1,0:T(8,128)(2,1)} %bitcast.14, bf16[128,768]{1,0:T(8,128)(2,1)} %seeds.1, bf16[2,64,768]{2,1,0:T(8,128)(2,1)} %bitcast.15, s32[1,128]{1,0:T(1,128)} %bitcast.17, f32[64,128]{1,0:T(8,128)} %bitcast.16, ...), custom_call_target="tpu_custom_call" | custom-call | flops 6499999744 | bytes 8000000 | tf_op jit(solution)/shard_map/pallas_call | solution.py:475
  96.4 0.0 copy-start.1
  96.4 2.5 %convert_element_type.2 = f32[512,768]{1,0:T(8,128)} convert(bf16[512,768]{1,0:T(8,128)(2,1)} %get-tuple-element.5) | non-fusion elementwise | flops 393216 | bytes 2359296 | tf_op jit(solution)/shard_map/convert_element_type | solution.py:509
  98.9 0.0 copy-done.1
  98.9 1.0 %convert_bitcast_fusion = f32[3840,64]{0,1:T(8,128)} fusion(bf16[64,5376]{1,0:T(8,128)(2,1)S(1)} %copy-done.1), kind=kLoop, calls=%fused_computation | loop fusion | flops 245760 | bytes 1474560 | tf_op jit(solution)/shard_map/transpose | solution.py:507
  99.9 0.8 maximum_convert_fusion
  (3 shorter events, 0.0 us)
Async XLA Ops:
  0.6 2.0 %copy-start = (s32[128,5]{0,1:T(8,128)S(1)}, s32[128,5]{0,1:T(8,128)}, u32[]{:S(2)}) copy-start(s32[128,5]{0,1:T(8,128)} %param.15) | copy-start | bytes 7684
  96.4 2.5 %copy-start.1 = (bf16[64,5376]{1,0:T(8,128)(2,1)S(1)}, bf16[64,5376]{1,0:T(8,128)(2,1)}, u32[]{:S(2)}) copy-start(bf16[64,5376]{1,0:T(8,128)(2,1)} %get-tuple-element.6) | copy-start | bytes 2064388
